TPU v7x, 32 devices: a whole 2x2x4 slice. The times are simulated.
32 devices in a mesh: dp: 4 (over y, core), wide: 4 (over z), narrow: 2 (over x).
Axes of the slice: x: 2, y: 2, z: 4, core: 2. Of those that a mesh axis runs over, the one named last changes fastest.
Arguments:
- streams: bfloat16 [4, 1024, 2048], P(None, 'dp', ('wide', 'narrow')), may hold values from -6 to 6
- prior: bfloat16 [12, 1024, 2048], P(None, 'dp', ('wide', 'narrow')), may hold values from -6 to 6
- streams_grad: bfloat16 [4, 1024, 2048], P(None, 'dp', ('wide', 'narrow')), may hold values from -6 to 6
- w_qkv: bfloat16 [3, 2048, 2048], P(None, 'wide', 'narrow')
- qkv_bias: bfloat16 [3, 2048], P(None, ('narrow', 'wide')), may hold values from -3 to 3
- w_out: bfloat16 [2048, 2048], P('narrow', 'wide'), may hold values from -1.5 to 1.5
- w_up: bfloat16 [2048, 8192], P('wide', 'narrow')
- up_bias: bfloat16 [8192], P(('narrow', 'wide')), may hold values from -3 to 3
- w_down: bfloat16 [8192, 2048], P('narrow', 'wide'), may hold values from -0.0625 to 0.0625
- branch_bias: bfloat16 [2048], P(('wide', 'narrow')), may hold values from -3 to 3
- norm_gain: bfloat16 [4, 2048], P(None, ('wide', 'narrow')), may hold values from 0.25 to 1.75
- norm_bias: bfloat16 [4, 2048], P(None, ('wide', 'narrow')), may hold values from -2 to 2
- mix_gain: bfloat16 [2048], P(('wide', 'narrow')), may hold values from 0.099609375 to 1.8984375
- mix_in: bfloat16 [2048, 52], P(('wide', 'narrow')), may hold values from -0.125 to 0.125
- mix_out: bfloat16 [52, 52], replicated, may hold values from -0.875 to 0.875
- mix_static: bfloat16 [52], replicated, may hold values from -3 to 3
Outputs:
- streams_out: bfloat16 [4, 1024, 2048], P(None, 'dp', ('wide', 'narrow'))
- streams_in_grad: bfloat16 [4, 1024, 2048], P(None, 'dp', ('wide', 'narrow'))
- prior_grad: bfloat16 [12, 1024, 2048], P(None, 'dp', ('wide', 'narrow'))
- w_qkv_grad: float32 [3, 2048, 2048], P(None, 'wide', 'narrow')
- qkv_bias_grad: float32 [3, 2048], P(None, ('narrow', 'wide'))
- w_out_grad: float32 [2048, 2048], P('narrow', 'wide')
- w_up_grad: float32 [2048, 8192], P('wide', 'narrow')
- up_bias_grad: float32 [8192], P(('narrow', 'wide'))
- w_down_grad: float32 [8192, 2048], P('narrow', 'wide')
- branch_bias_grad: float32 [2048], P(('wide', 'narrow'))
- norm_gain_grad: float32 [4, 2048], P(None, ('wide', 'narrow'))
- norm_bias_grad: float32 [4, 2048], P(None, ('wide', 'narrow'))
- mix_gain_grad: float32 [2048], P(('wide', 'narrow'))
- mix_in_grad: float32 [2048, 52], P(('wide', 'narrow'))
- mix_out_grad: float32 [52, 52], replicated
- mix_static_grad: float32 [52], replicated
All inputs are finite; a program needn't handle non-finite values.
Results may differ from a plain program's by a relative error of at most 0.02.
Values may be sent and summed in bfloat16 or wider, within the bound.
No kernel may reach another device: no remote copies, remote signals or barrier semaphores. Data moves between devices by JAX's collectives and lax.ppermute only.
A program may use at most 192 MiB of HBM per device.

v0:
```python
import math
import jax
import jax.numpy as jnp
from jax import lax
from jax.sharding import PartitionSpec as P

D = 2048
HD = 128
ROT = 32
MIXH = 52
STACK = 13
norm_eps = 1e-05
rms_eps = 1e-06


def model_sum(parts):
    return lax.psum(parts, ("wide", "narrow"))


def gelu_exact(inputs):
    return 0.5 * inputs * (1.0 + lax.erf(inputs * (1.0 / math.sqrt(2.0))))


def gelu_slope(inputs):
    normal_cdf = 0.5 * (1.0 + lax.erf(inputs * (1.0 / math.sqrt(2.0))))
    return normal_cdf + inputs * jnp.exp(-0.5 * inputs * inputs) * (1.0 / math.sqrt(2.0 * math.pi))


def rotate(heads_in, cosine, sine_table, direction):
    half = ROT // 2
    first = heads_in[..., :half]
    second = heads_in[..., half:ROT]
    rest_part = heads_in[..., ROT:]
    cos_b = cosine[:, None, :]
    sin_b = direction * sine_table[:, None, :]
    return jnp.concatenate(
        [first * cos_b - second * sin_b, second * cos_b + first * sin_b, rest_part], axis=-1
    )


def masked_scores(query_rows, key_heads, row_start, row_block, length, scale):
    scores = (
        jnp.einsum("qhd,khd->hqk", query_rows, key_heads, preferred_element_type=jnp.float32)
        * scale
    )
    row_ids = row_start + lax.broadcasted_iota(jnp.int32, (row_block, length), 0)
    col_ids = lax.broadcasted_iota(jnp.int32, (row_block, length), 1)
    return jnp.where((col_ids <= row_ids)[None], scores, -1e30)


def attend_rows(queries, key_heads, value_heads, scale):
    length = queries.shape[0]
    row_block = min(512, length)

    def one_block(block_index):
        row_start = block_index * row_block
        scores = masked_scores(queries, key_heads, row_start, row_block, length, scale)
        row_top = jnp.max(scores, axis=2, keepdims=True)
        log_total = row_top + jnp.log(jnp.sum(jnp.exp(scores - row_top), axis=2, keepdims=True))
        attn_probs = jnp.exp(scores - log_total).astype(jnp.bfloat16)
        output = jnp.einsum(
            "hqk,khd->qhd", attn_probs, value_heads, preferred_element_type=jnp.float32
        )
        return (output, log_total[:, :, 0])

    outputs, totals = lax.map(one_block, jnp.arange(length // row_block, dtype=jnp.int32))
    return (outputs.reshape(queries.shape), totals)


def attend_back(queries, key_heads, value_heads, out_grad, totals, scale):
    length = queries.shape[0]
    row_block = min(512, length)

    def one_block(carry, block_index):
        key_grad, value_grad = carry
        row_start = block_index * row_block
        log_total = lax.dynamic_index_in_dim(totals, block_index, 0, keepdims=False)
        scores = masked_scores(queries, key_heads, row_start, row_block, length, scale)
        attn_probs = jnp.exp(scores - log_total[:, :, None])
        probs_low = attn_probs.astype(jnp.bfloat16)
        value_grad = value_grad + jnp.einsum(
            "hqk,qhd->khd", probs_low, out_grad, preferred_element_type=jnp.float32
        )
        prob_grad = jnp.einsum(
            "qhd,khd->hqk", out_grad, value_heads, preferred_element_type=jnp.float32
        )
        row_dot = jnp.sum(attn_probs * prob_grad, axis=2, keepdims=True)
        score_grad = (attn_probs * (prob_grad - row_dot)).astype(jnp.bfloat16)
        query_grad = (
            jnp.einsum("hqk,khd->qhd", score_grad, key_heads, preferred_element_type=jnp.float32)
            * scale
        )
        key_grad = (
            key_grad
            + jnp.einsum("hqk,qhd->khd", score_grad, queries, preferred_element_type=jnp.float32)
            * scale
        )
        return ((key_grad, value_grad), query_grad)

    zero_heads = jnp.zeros(queries.shape, jnp.float32)
    (key_grad, value_grad), query_blocks = lax.scan(
        one_block, (zero_heads, zero_heads), jnp.arange(length // row_block, dtype=jnp.int32)
    )
    return (query_blocks.reshape(queries.shape), key_grad, value_grad)


def contract_rows(left, right):
    return lax.dot_general(
        left, right, (((0,), (0,)), ((), ())), preferred_element_type=jnp.float32
    )


def contract_cols(left, right):
    return lax.dot_general(
        left, right, (((1,), (1,)), ((), ())), preferred_element_type=jnp.float32
    )


def per_device(
    streams,
    prior,
    streams_grad,
    w_qkv,
    qkv_bias,
    w_out,
    w_up,
    up_bias,
    w_down,
    branch_bias,
    norm_gain,
    norm_bias,
    mix_gain,
    mix_in,
    mix_out,
    mix_static,
):
    high = lax.Precision.HIGHEST
    length = streams.shape[1]
    local_cols = streams.shape[2]
    heads_here = local_cols // HD
    scale = 1.0 / math.sqrt(HD)
    inputs = streams.astype(jnp.float32)
    row_total, row_squares = model_sum((jnp.sum(inputs, axis=2), jnp.sum(inputs * inputs, axis=2)))
    row_mean = row_total / D
    inv_std = lax.rsqrt(row_squares / D - row_mean * row_mean + norm_eps)
    centred = (inputs - row_mean[:, :, None]) * inv_std[:, :, None]
    norm_scale = norm_gain.astype(jnp.float32)[:, None, :]
    normed = (centred * norm_scale + norm_bias.astype(jnp.float32)[:, None, :]).astype(jnp.bfloat16)
    near_cols = lax.all_gather(normed, "narrow", axis=2, tiled=True)
    qkv_part = jnp.einsum("std,sdf->stf", near_cols[:3], w_qkv, preferred_element_type=jnp.float32)
    up_part = jnp.dot(near_cols[3], w_up, preferred_element_type=jnp.float32)
    qkv_pre, up_summed = (
        lax.psum_scatter(qkv_part, "wide", scatter_dimension=2, tiled=True),
        lax.psum_scatter(up_part[None], "wide", scatter_dimension=2, tiled=True),
    )
    up_pre = up_summed[0]
    qkv_pre = qkv_pre + qkv_bias.astype(jnp.float32)[:, None, :]
    up_pre = up_pre + up_bias.astype(jnp.float32)[None, :]
    positions = lax.iota(jnp.float32, length)
    freqs = jnp.exp(lax.iota(jnp.float32, ROT // 2) * (-2.0 * math.log(10000.0) / ROT))
    angles = positions[:, None] * freqs[None, :]
    cosine = jnp.cos(angles)
    sine_table = jnp.sin(angles)
    head_view = qkv_pre.reshape(3, length, heads_here, HD)
    queries = rotate(head_view[0], cosine, sine_table, 1.0).astype(jnp.bfloat16)
    key_heads = rotate(head_view[1], cosine, sine_table, 1.0).astype(jnp.bfloat16)
    value_heads = head_view[2].astype(jnp.bfloat16)
    attn_heads, totals = attend_rows(queries, key_heads, value_heads, scale)
    attn_low = attn_heads.reshape(length, local_cols).astype(jnp.bfloat16)
    hidden = gelu_exact(up_pre).astype(jnp.bfloat16)
    attn_wide, hidden_wide = (
        lax.all_gather(attn_low, "wide", axis=1, tiled=True),
        lax.all_gather(hidden, "wide", axis=1, tiled=True),
    )
    branch_part = jnp.dot(attn_wide, w_out, preferred_element_type=jnp.float32) + jnp.dot(
        hidden_wide, w_down, preferred_element_type=jnp.float32
    )
    branch = (
        lax.psum_scatter(branch_part, "narrow", scatter_dimension=1, tiled=True)
        + branch_bias.astype(jnp.float32)[None, :]
    )
    layer_out = inputs[3] + branch
    mix_scale = mix_gain.astype(jnp.float32)
    scaled = layer_out * mix_scale[None, :]
    mix_weight = mix_in.astype(jnp.float32)
    mix_back = mix_out.astype(jnp.float32)
    energy, logit_sum = model_sum(
        (jnp.sum(layer_out * layer_out, axis=1), jnp.dot(scaled, mix_weight, precision=high))
    )
    rms = lax.rsqrt(energy / D + rms_eps)
    logits = logit_sum * rms[:, None]
    mix_hidden = gelu_exact(logits)
    weights = (
        jnp.dot(mix_hidden, mix_back, precision=high) + mix_static.astype(jnp.float32)[None, :]
    )
    coef = weights.reshape(length, 4, STACK)
    prior_vals = prior.astype(jnp.float32)
    mixed = jnp.einsum("tsj,jtl->stl", coef[:, :, : STACK - 1], prior_vals, precision=high)
    streams_out = (
        mixed + jnp.transpose(coef[:, :, STACK - 1])[:, :, None] * layer_out[None]
    ).astype(jnp.bfloat16)
    grad_out = streams_grad.astype(jnp.float32)
    prior_part = jnp.einsum("stl,jtl->tsj", grad_out, prior_vals, precision=high)
    layer_part = jnp.einsum("stl,tl->ts", grad_out, layer_out, precision=high)
    coef_part = jnp.concatenate([prior_part, layer_part[:, :, None]], axis=2).reshape(length, MIXH)
    (coef_grad,) = model_sum((coef_part,))
    prior_grad = jnp.einsum(
        "tsj,stl->jtl", coef[:, :, : STACK - 1], grad_out, precision=high
    ).astype(jnp.bfloat16)
    layer_grad = jnp.einsum("ts,stl->tl", coef[:, :, STACK - 1], grad_out, precision=high)
    static_grad = jnp.sum(coef_grad, axis=0)
    mix_out_grad = jnp.dot(mix_hidden.T, coef_grad, precision=high)
    logit_grad = jnp.dot(coef_grad, mix_back.T, precision=high) * gelu_slope(logits)
    sum_grad = logit_grad * rms[:, None]
    rms_grad = jnp.sum(logit_grad * logit_sum, axis=1)
    energy_grad = -0.5 * rms_grad * rms * rms * rms / D
    mix_in_grad = jnp.dot(scaled.T, sum_grad, precision=high)
    scaled_grad = jnp.dot(sum_grad, mix_weight.T, precision=high)
    mix_gain_grad = jnp.sum(scaled_grad * layer_out, axis=0)
    layer_grad = (
        layer_grad + scaled_grad * mix_scale[None, :] + 2.0 * energy_grad[:, None] * layer_out
    )
    branch_grad = layer_grad.astype(jnp.bfloat16)
    branch_bias_grad = jnp.sum(branch_grad.astype(jnp.float32), axis=0)
    branch_near = lax.all_gather(branch_grad, "narrow", axis=1, tiled=True)
    attn_grad, hidden_grad = (
        lax.psum_scatter(
            contract_cols(branch_near, w_out), "wide", scatter_dimension=1, tiled=True
        ),
        lax.psum_scatter(
            contract_cols(branch_near, w_down), "wide", scatter_dimension=1, tiled=True
        ),
    )
    out_weight_grad = contract_rows(attn_wide, branch_near)
    down_weight_grad = contract_rows(hidden_wide, branch_near)
    attn_low_grad = attn_grad.astype(jnp.bfloat16).reshape(length, heads_here, HD)
    up_grad = (hidden_grad * gelu_slope(up_pre)).astype(jnp.bfloat16)
    up_bias_grad = jnp.sum(up_grad.astype(jnp.float32), axis=0)
    query_grad, key_grad, value_grad = attend_back(
        queries, key_heads, value_heads, attn_low_grad, totals, scale
    )
    query_pre = rotate(query_grad, cosine, sine_table, -1.0).reshape(length, local_cols)
    key_pre = rotate(key_grad, cosine, sine_table, -1.0).reshape(length, local_cols)
    projected_grad = jnp.stack([query_pre, key_pre, value_grad.reshape(length, local_cols)]).astype(
        jnp.bfloat16
    )
    qkv_bias_grad = jnp.sum(projected_grad.astype(jnp.float32), axis=1)
    far_qkv, far_up = (
        lax.all_gather(projected_grad, "wide", axis=2, tiled=True),
        lax.all_gather(up_grad[None], "wide", axis=2, tiled=True),
    )
    qkv_weight_grad = jnp.einsum(
        "std,stf->sdf", near_cols[:3], far_qkv, preferred_element_type=jnp.float32
    )
    up_weight_grad = contract_rows(near_cols[3], far_up[0])
    normed_part = jnp.concatenate(
        [
            jnp.einsum("stf,sdf->std", far_qkv, w_qkv, preferred_element_type=jnp.float32),
            contract_cols(far_up[0], w_up)[None],
        ],
        axis=0,
    )
    normed_grad = lax.psum_scatter(normed_part, "narrow", scatter_dimension=2, tiled=True)
    gain_grad = jnp.sum(normed_grad * centred, axis=1)
    shift_grad = jnp.sum(normed_grad, axis=1)
    centred_grad = normed_grad * norm_scale
    grad_total, grad_cross = model_sum(
        (jnp.sum(centred_grad, axis=2), jnp.sum(centred_grad * centred, axis=2))
    )
    input_grad = inv_std[:, :, None] * (
        centred_grad - (grad_total / D)[:, :, None] - centred * (grad_cross / D)[:, :, None]
    )
    input_grad = input_grad.at[3].add(layer_grad)
    streams_in_grad = input_grad.astype(jnp.bfloat16)
    summed = lax.psum(
        (
            qkv_weight_grad,
            qkv_bias_grad,
            out_weight_grad,
            up_weight_grad,
            up_bias_grad,
            down_weight_grad,
            branch_bias_grad,
            gain_grad,
            shift_grad,
            mix_gain_grad,
            mix_in_grad,
            mix_out_grad,
            static_grad,
        ),
        "dp",
    )
    return (
        streams_out,
        streams_in_grad,
        prior_grad,
        summed[0],
        summed[1],
        summed[2],
        summed[3],
        summed[4],
        summed[5],
        summed[6],
        summed[7],
        summed[8],
        summed[9],
        summed[10],
        summed[11],
        summed[12],
    )


def solution(mesh):
    return jax.shard_map(
        per_device,
        mesh=mesh,
        in_specs=(
            P(None, "dp", ("wide", "narrow")),
            P(None, "dp", ("wide", "narrow")),
            P(None, "dp", ("wide", "narrow")),
            P(None, "wide", "narrow"),
            P(None, ("narrow", "wide")),
            P("narrow", "wide"),
            P("wide", "narrow"),
            P(("narrow", "wide")),
            P("narrow", "wide"),
            P(("wide", "narrow")),
            P(None, ("wide", "narrow")),
            P(None, ("wide", "narrow")),
            P(("wide", "narrow")),
            P(("wide", "narrow"), None),
            P(),
            P(),
        ),
        out_specs=(
            P(None, "dp", ("wide", "narrow")),
            P(None, "dp", ("wide", "narrow")),
            P(None, "dp", ("wide", "narrow")),
            P(None, "wide", "narrow"),
            P(None, ("narrow", "wide")),
            P("narrow", "wide"),
            P("wide", "narrow"),
            P(("narrow", "wide")),
            P("narrow", "wide"),
            P(("wide", "narrow")),
            P(None, ("wide", "narrow")),
            P(None, ("wide", "narrow")),
            P(("wide", "narrow")),
            P(("wide", "narrow"), None),
            P(),
            P(),
        ),
        check_vma=False,
    )
```

profile of v0, /device:TPU:0, one launch (start us, length us, event | category | flops | bytes accessed | tf_op | source)
XLA Modules:
  0.0 1101.8 jit_solution(11456983785825005663)
XLA Ops:
  7.2 1.5 convert_reduce_fusion.2
  10.2 23.3 %all-reduce.2 = (f32[4,256]{1,0:T(4,128)S(1)}, f32[4,256]{1,0:T(4,128)S(1)}) all-reduce(f32[4,256]{1,0:T(4,128)S(1)} %get-tuple-element.142, f32[4,256]{1,0:T(4,128)S(1)} %get-tuple-element.141), channel_id=1, replica_groups=mesh['dp'=4,'wide'=4,'narrow'=2] {'wide','narrow'}, use_global_device_ids=true, to_apply=%region_3.0 | all-reduce | flops 2048 | bytes 16384 | tf_op jit(solution)/shard_map/psum | solution.py:17
  33.5 2.2 add_convert_fusion
  35.8 18.7 %all-gather.6.cloned.1.call-done = bf16[4,256,512]{2,1,0:T(8,128)(2,1)} async-done(((bf16[4,256,256]{2,1,0:T(8,128)(2,1)}), bf16[4,256,512]{2,1,0:T(8,128)(2,1)}) %all-gather.6.cloned.1.call-update) | async-done | bytes 1048592 | tf_op jit(solution)/shard_map/all_gather | solution.py:149
  54.4 5.6 convolution_bitcast_fusion
  60.1 3.8 fusion.72
  64.6 72.4 %reduce-scatter.9.cloned.1.call-done = f32[1,256,1024]{2,1,0:T(8,128)} async-done(((f32[1,256,4096]{2,1,0:T(8,128)}), f32[1,256,1024]{2,1,0:T(8,128)}) %reduce-scatter.9.cloned.1.call-update) | async-done | bytes 1048592 | tf_op jit(solution)/shard_map/reduce_scatter | solution.py:154
  136.9 2.2 multiply_convert_fusion
  141.1 59.6 %reduce-scatter.7.cloned.1.call-done = f32[3,256,256]{2,1,0:T(8,128)} async-done(((f32[3,256,1024]{2,1,0:T(8,128)}), f32[3,256,256]{2,1,0:T(8,128)}) %reduce-scatter.7.cloned.1.call-update) | async-done | bytes 786448 | tf_op jit(solution)/shard_map/reduce_scatter | solution.py:153
  204.5 1.8 squeeze.37
  209.0 1.6 convert_element_type.95
  210.6 1.7 fusion.63
  214.0 22.1 %all_gather.19 = bf16[256,1024]{0,1:T(8,128)(2,1)} all-gather(bf16[256,256]{0,1:T(8,128)(2,1)S(1)} %bitcast.112), channel_id=1, replica_groups=mesh['dp'=4,'wide'=4,'narrow'=2] {'wide'}, dimensions={1}, use_global_device_ids=true | all-gather | bytes 655360 | tf_op jit(solution)/shard_map/all_gather | solution.py:172
  236.2 20.9 %all-gather.8.cloned.1.call-done = bf16[256,4096]{1,0:T(8,128)(2,1)} async-done(((bf16[256,1024]{1,0:T(8,128)(2,1)}), bf16[256,4096]{1,0:T(8,128)(2,1)}) %all-gather.8.cloned.1.call-update) | async-done | bytes 2097168 | tf_op jit(solution)/shard_map/all_gather | solution.py:173
  257.1 4.2 fusion.66
  261.3 1.3 convolution_add_fusion
  262.6 2.1 convert_element_type.90
  265.9 3.7 fusion
  269.6 6.5 reduce-scatter.11.cloned.1.call-done
  276.1 1.8 multiply_reduce_fusion.6
  277.9 2.6 convolution_bitcast_fusion.2
  281.7 1.9 copy.142
  283.5 1.5 reshape.183
  285.0 1.6 fusion.29
  288.1 68.3 %all-reduce.9.cloned.1.call-done = (f32[256,52]{0,1:T(8,128)}, f32[256]{0:T(256)}, f32[256,52]{0,1:T(8,128)}) async-done(((f32[256,52]{0,1:T(8,128)}, f32[256]{0:T(256)}, f32[256,52]{0,1:T(8,128)}), (f32[256,52]{0,1:T(8,128)}, f32[256]{0:T(256)}, f32[256,52]{0,1:T(8,128)})) %all-reduce.9.cloned.1.call-update) | async-done | bytes 107536 | tf_op jit(solution)/shard_map/psum | solution.py:17
  357.0 1.7 multiply_reduce_fusion.7
  359.9 1.7 convolution_add_fusion.1
  361.6 1.5 reshape.182
  363.0 1.4 slice.127
  364.4 1.5 copy.175
  365.9 2.4 fusion.34
  368.3 2.4 convert_reduce_fusion.3
  370.7 5.6 all_gather.21
  376.4 1.4 fusion.67
  377.9 5.5 fusion.69
  383.4 21.7 %reduce-scatter.13.cloned.1.call-done = f32[256,256]{1,0:T(8,128)} async-done(((f32[256,1024]{1,0:T(8,128)}), f32[256,256]{1,0:T(8,128)}) %reduce-scatter.13.cloned.1.call-update) | async-done | bytes 262160 | tf_op jit(solution)/shard_map/reduce_scatter | solution.py:227
  405.1 1.6 convert_element_type.107
  406.8 1.7 copy.178
  408.5 1.5 multiply_reduce_fusion.4
  416.2 1.8 pad_maximum_fusion.6
  419.8 2.0 convolution_convert_fusion
  422.9 2.4 convert_reduce_fusion.1
  425.3 58.1 %reduce-scatter.15.cloned.1.call-done = f32[256,1024]{1,0:T(8,128)} async-done(((f32[256,4096]{1,0:T(8,128)}), f32[256,1024]{1,0:T(8,128)}) %reduce-scatter.15.cloned.1.call-update) | async-done | bytes 1048592 | tf_op jit(solution)/shard_map/reduce_scatter | solution.py:230
  483.5 3.4 convert_reduce_fusion
  487.0 36.9 %all-gather.10.cloned.1.call-done = bf16[3,256,1024]{2,1,0:T(8,128)(2,1)} async-done(((bf16[3,256,256]{2,1,0:T(8,128)(2,1)}), bf16[3,256,1024]{2,1,0:T(8,128)(2,1)}) %all-gather.10.cloned.1.call-update) | async-done | bytes 1572880 | tf_op jit(solution)/shard_map/all_gather | solution.py:249
  523.9 3.6 fusion.68
  527.5 42.7 %all-gather.12.cloned.1.call-done = bf16[256,4096]{1,0:T(8,128)(2,1)} async-done(((bf16[256,1024]{1,0:T(8,128)(2,1)}), bf16[256,4096]{1,0:T(8,128)(2,1)}) %all-gather.12.cloned.1.call-update) | async-done | bytes 2097168 | tf_op jit(solution)/shard_map/all_gather | solution.py:250
  570.2 4.1 convolution_bitcast_fusion.1
  574.3 1.5 pad_maximum_fusion
  579.0 1.8 fusion.70
  580.9 4.7 fusion.71
  585.6 3.8 fusion.73
  589.4 17.2 %reduce-scatter.17.cloned.1.call-done = f32[4,256,256]{2,1,0:T(8,128)} async-done(((f32[4,256,512]{2,1,0:T(8,128)}), f32[4,256,256]{2,1,0:T(8,128)}) %reduce-scatter.17.cloned.1.call-update) | async-done | bytes 1048592 | tf_op jit(solution)/shard_map/reduce_scatter | solution.py:263
  606.6 2.6 multiply_reduce_fusion
  609.3 5.6 fusion.31
  616.8 3.3 convert_bitcast_fusion
  620.1 1.7 copy.161
  621.9 3.7 fusion.10
  626.4 20.7 %all-reduce = (f32[4,256]{1,0:T(4,128)S(1)}, f32[4,256]{1,0:T(4,128)S(1)}) all-reduce(f32[4,256]{1,0:T(4,128)S(1)} %get-tuple-element.138, f32[4,256]{1,0:T(4,128)S(1)} %get-tuple-element.139), channel_id=1, replica_groups=mesh['dp'=4,'wide'=4,'narrow'=2] {'wide','narrow'}, use_global_device_ids=true, to_apply=%region_21.22 | all-reduce | flops 2048 | bytes 16384 | tf_op jit(solution)/shard_map/psum | solution.py:17
  648.8 423.5 %all-reduce.13.cloned.1.call-done = (f32[3,512,1024]{2,1,0:T(8,128)}, f32[1024,512]{1,0:T(8,128)}, f32[512,4096]{1,0:T(8,128)}, f32[4096,512]{1,0:T(8,128)}) async-done(((f32[3,512,1024]{2,1,0:T(8,128)}, f32[1024,512]{1,0:T(8,128)}, f32[512,4096]{1,0:T(8,128)}, f32[4096,512]{1,0:T(8,128)}), (f32[3,512,1024]{2,1,0:T(8,128)}, f32[1024,512]{1,0:T(8,128)}, f32[512,4096]{1,0:T(8,128)}, ...) | async-done | bytes 25165840 | tf_op jit(solution)/shard_map/psum | solution.py:275
  1072.3 7.1 copy.244
  1079.9 1.3 copy.246
  1081.3 4.3 copy.247
  1087.3 3.9 copy.249
  (208 shorter events, 41.2 us)
Async XLA Ops:
  7.2 52.9 %copy-start = (bf16[3,512,1024]{2,1,0:T(8,128)(2,1)S(1)}, bf16[3,512,1024]{2,1,0:T(8,128)(2,1)}, u32[]{:S(2)}) copy-start(bf16[3,512,1024]{2,1,0:T(8,128)(2,1)} %param.21) | copy-start | bytes 9437188
  7.2 47.2 %all-gather.6.cloned.1.call-start = ((), (), s32[]{:S(2)}) async-start(), calls=%async_computation.6 | async-start | bytes 1572864 | tf_op jit(solution)/shard_map/all_gather | solution.py:149
  35.7 101.2 %reduce-scatter.9.cloned.1.call-start = ((), (), s32[]{:S(2)}) async-start(), calls=%async_computation.8 | async-start | bytes 5242880 | tf_op jit(solution)/shard_map/reduce_scatter | solution.py:154
  60.0 140.7 %reduce-scatter.7.cloned.1.call-start = ((), (), s32[]{:S(2)}) async-start(), calls=%async_computation.7 | async-start | bytes 3932160 | tf_op jit(solution)/shard_map/reduce_scatter | solution.py:153
  63.9 75.4 %copy-start.52 = (bf16[3,256]{1,0:T(4,128)(2,1)S(1)}, bf16[3,256]{1,0:T(4,128)(2,1)}, u32[]{:S(2)}) copy-start(bf16[3,256]{1,0:T(4,128)(2,1)} %param.22) | copy-start | bytes 4612
  63.9 193.2 %all-gather.8.cloned.1.call-start = ((), (), s32[]{:S(2)}) async-start(), calls=%async_computation.9 | async-start | bytes 2621440 | tf_op jit(solution)/shard_map/all_gather | solution.py:173
  64.6 138.0 %copy-start.41 = (f32[1024]{0:T(1024)}, f32[1024]{0:T(1024)S(1)}, u32[]{:S(2)}) copy-start(f32[1024]{0:T(1024)S(1)} %convert_element_type.100) | copy-start | bytes 12292
  139.2 136.9 %reduce-scatter.11.cloned.1.call-start = ((), (), s32[]{:S(2)}) async-start(), calls=%async_computation.10 | async-start | bytes 786432 | tf_op jit(solution)/shard_map/reduce_scatter | solution.py:179
  210.6 1.7 copy-start.32
  210.6 1.9 copy-start.26
  210.6 1.9 copy-start.28
  210.6 2.0 copy-start.36
  212.5 1.5 copy-start.17
  212.5 1.5 copy-start.19
  212.5 1.5 copy-start.21
  257.1 4.2 copy-start.6
  257.1 4.2 copy-start.11
  261.3 3.5 copy-start.55
  261.3 4.0 copy-start.56
  262.6 93.8 %all-reduce.9.cloned.1.call-start = ((), (), s32[]{:S(2)}) async-start(), calls=%async_computation.16 | async-start | bytes 231424 | tf_op jit(solution)/shard_map/psum | solution.py:17
  276.1 4.4 copy-start.33
  277.9 90.4 %copy-start.9 = (f32[256,256]{1,0:T(8,128)}, f32[256,256]{1,0:T(8,128)S(1)}, u32[]{:S(2)}) copy-start(f32[256,256]{1,0:T(8,128)S(1)} %get-tuple-element.171) | copy-start | bytes 786436
  286.7 118.5 %reduce-scatter.13.cloned.1.call-start = ((), (), s32[]{:S(2)}) async-start(), calls=%async_computation.11 | async-start | bytes 1310720 | tf_op jit(solution)/shard_map/reduce_scatter | solution.py:227
  357.0 2.9 copy-start.44
  365.9 10.5 copy-start.12
  377.8 105.6 %reduce-scatter.15.cloned.1.call-start = ((), (), s32[]{:S(2)}) async-start(), calls=%async_computation.13 | async-start | bytes 5242880 | tf_op jit(solution)/shard_map/reduce_scatter | solution.py:230
  383.4 140.5 %all-gather.10.cloned.1.call-start = ((), (), s32[]{:S(2)}) async-start(), calls=%async_computation.12 | async-start | bytes 1966080 | tf_op jit(solution)/shard_map/all_gather | solution.py:249
  408.4 2.7 copy-start.22
  408.4 2.7 copy-start.24
  408.4 2.7 copy-start.29
  408.4 3.2 copy-start.18
  408.4 3.2 copy-start.20
  408.5 3.2 copy-start.27
  409.9 2.8 copy-start.31
  425.3 144.9 %all-gather.12.cloned.1.call-start = ((), (), s32[]{:S(2)}) async-start(), calls=%async_computation.15 | async-start | bytes 2621440 | tf_op jit(solution)/shard_map/all_gather | solution.py:250
  486.9 119.6 %reduce-scatter.17.cloned.1.call-start = ((), (), s32[]{:S(2)}) async-start(), calls=%async_computation.14 | async-start | bytes 3145728 | tf_op jit(solution)/shard_map/reduce_scatter | solution.py:263
  527.5 46.8 %copy-start.5 = (f32[3,256,512]{2,1,0:T(8,128)S(1)}, f32[3,256,512]{2,1,0:T(8,128)}, u32[]{:S(2)}) copy-start(f32[3,256,512]{2,1,0:T(8,128)} %fusion.68) | copy-start | bytes 4718596
  575.8 2.3 copy-start.10
  575.8 2.3 copy-start.39
  575.8 2.3 copy-start.46
  575.9 3.2 copy-start.7
  575.9 5.0 copy-start.13
  575.9 72.9 %all-reduce.11.cloned.1.call-start = ((), (), s32[]{:S(2)}) async-start(), calls=%async_computation.17 | async-start | bytes 209920 | tf_op jit(solution)/shard_map/psum | solution.py:275
  580.9 4.7 copy-start.16
  580.9 4.7 copy-start.34
  585.6 21.0 %copy-start.3 = (bf16[4,256,256]{2,1,0:T(8,128)(2,1)S(1)}, bf16[4,256,256]{2,1,0:T(8,128)(2,1)}, u32[]{:S(2)}) copy-start(bf16[4,256,256]{2,1,0:T(8,128)(2,1)} %param.18) | copy-start | bytes 1572868
  585.6 23.7 %copy-start.15 = (bf16[256,4096]{1,0:T(8,128)(2,1)S(1)}, bf16[256,4096]{1,0:T(8,128)(2,1)}, u32[]{:S(2)}) copy-start(bf16[256,4096]{1,0:T(8,128)(2,1)} %all-gather.12.cloned.1.call-done) | copy-start | bytes 6291460
  609.2 463.0 %all-reduce.13.cloned.1.call-start = ((), (), s32[]{:S(2)}) async-start(), calls=%async_computation.18 | async-start | bytes 50331648 | tf_op jit(solution)/shard_map/psum | solution.py:275
  621.9 25.3 %copy-start.8 = (f32[4,256,256]{2,1,0:T(8,128)S(1)}, f32[4,256,256]{2,1,0:T(8,128)}, u32[]{:S(2)}) copy-start(f32[4,256,256]{2,1,0:T(8,128)} %reduce-scatter.17.cloned.1.call-done) | copy-start | bytes 3145732
  625.5 22.3 %copy-start.30 = (f32[256,256]{1,0:T(8,128)S(1)}, f32[256,256]{1,0:T(8,128)}, u32[]{:S(2)}) copy-start(f32[256,256]{1,0:T(8,128)} %get-tuple-element.165) | copy-start | bytes 786436
  1072.2 7.1 copy-start.50
  1072.3 7.7 copy-start.14
  1072.3 9.0 copy-start.4
  1079.9 6.2 slice-start
  1081.2 4.3 copy-start.49
  1081.2 6.0 slice-start.1
  1087.2 4.0 copy-start.54
  1087.2 4.5 copy-start.48
  1087.2 5.1 copy-start.47
  1087.2 5.7 copy-start.53
  1087.3 6.3 copy-start.40
  1087.3 6.9 copy-start.43
  1087.3 7.5 copy-start.57
  1087.3 8.0 copy-start.1
  (9 other events, 9.7 us)
Sparse Core Ops, SparseCore 0:
  35.8 18.5 all-gather.5
  60.1 76.7 reduce-scatter.8
  139.9 60.7 reduce-scatter.6
  202.8 54.2 all-gather.7
  262.7 13.3 reduce-scatter.10
  286.8 69.5 all-reduce.8
  377.9 27.1 reduce-scatter.12
  408.0 75.4 reduce-scatter.14
  485.7 38.1 all-gather.9
  526.0 44.1 all-gather.11
  576.0 30.5 reduce-scatter.16
  610.6 30.8 all-reduce.10
  645.6 426.6 all-reduce.12
where the time goes:
time: 1100 us
  waiting for transfers between devices  847 us (77%)
  matrix products  75 us (7%)
  blocking collectives  71.8 us (7%)
  local copies, waits for them, and re-layouts  54.5 us (5%)
  other arithmetic  38.3 us (3%)
  between operations  14.6 us (1%)
    psum x2, waiting for transfers between devices, per_device(): lax.psum((qkv_weight_grad, qkv_bias_grad, out_weight_grad, up_weight_grad...  423 us
    reduce_scatter x1, waiting for transfers between devices, per_device(): lax.psum_scatter(up_part[None], 'wide', scatter_dimension=2, tiled=True)  72.4 us
    psum x1, waiting for transfers between devices, model_sum(): return lax.psum(parts, ('wide', 'narrow'))  68.3 us
    reduce_scatter x1, waiting for transfers between devices, per_device(): lax.psum_scatter(qkv_part, 'wide', scatter_dimension=2, tiled=True)  59.6 us
    reduce_scatter x1, waiting for transfers between devices, per_device(): lax.psum_scatter(contract_cols(branch_near, w_down), 'wide', scatter_dime...  58.1 us
    psum x2, blocking collectives, model_sum(): return lax.psum(parts, ('wide', 'narrow'))  44 us
    all_gather x1, waiting for transfers between devices, per_device(): lax.all_gather(up_grad[None], 'wide', axis=2, tiled=True)  42.7 us
    all_gather x1, waiting for transfers between devices, per_device(): lax.all_gather(projected_grad, 'wide', axis=2, tiled=True)  36.9 us
  transfers between devices with their start and end apart: 13, of which 12 were waited for; matrix products, arithmetic and copies ran while one was open for 8% of the time, Pallas kernels for 0%

commit v1 on v0

--- a/solution.py
+++ b/solution.py
@@ -14,7 +14,7 @@
 
 
 def model_sum(parts):
-    return lax.psum(parts, ("wide", "narrow"))
+    return lax.psum(lax.psum(parts, axis_name="narrow"), axis_name="wide")
 
 
 def gelu_exact(inputs):

time: 1100 us -> 1090 us (level)
    psum x1 -> x2, waiting for transfers between devices: 68.3 us -> 57.4 us  [model_sum(): return lax.psum(lax.psum(parts, axis_name='narrow'), axis_name='wide')]
    psum x2 -> x4, blocking collectives: 44 us -> 35.3 us  [model_sum(): return lax.psum(lax.psum(parts, axis_name='narrow'), axis_name='wide')]
  transfers between devices with their start and end apart: 13 -> 14, of which waited for: 12 -> 13; matrix products, arithmetic and copies ran while one was open for 8% -> 8% of each run, Pallas kernels for 0% -> 0%
where the time goes in v1:
time: 1090 us
  waiting for transfers between devices  841 us (77%)
  matrix products  75 us (7%)
  blocking collectives  63.1 us (6%)
  local copies, waits for them, and re-layouts  54.5 us (5%)
  other arithmetic  38.3 us (4%)
  between operations  14.6 us (1%)
    psum x2, waiting for transfers between devices, per_device(): lax.psum((qkv_weight_grad, qkv_bias_grad, out_weight_grad, up_weight_grad...  427 us
    reduce_scatter x1, waiting for transfers between devices, per_device(): lax.psum_scatter(up_part[None], 'wide', scatter_dimension=2, tiled=True)  72.4 us
    reduce_scatter x1, waiting for transfers between devices, per_device(): lax.psum_scatter(qkv_part, 'wide', scatter_dimension=2, tiled=True)  59.6 us
    reduce_scatter x1, waiting for transfers between devices, per_device(): lax.psum_scatter(contract_cols(branch_near, w_down), 'wide', scatter_dime...  58.2 us
    psum x2, waiting for transfers between devices, model_sum(): return lax.psum(lax.psum(parts, axis_name='narrow'), axis_name='wide')  57.4 us
    all_gather x1, waiting for transfers between devices, per_device(): lax.all_gather(up_grad[None], 'wide', axis=2, tiled=True)  42.9 us
    all_gather x1, waiting for transfers between devices, per_device(): lax.all_gather(projected_grad, 'wide', axis=2, tiled=True)  36.8 us
    psum x4, blocking collectives, model_sum(): return lax.psum(lax.psum(parts, axis_name='narrow'), axis_name='wide')  35.3 us
  transfers between devices with their start and end apart: 14, of which 13 were waited for; matrix products, arithmetic and copies ran while one was open for 8% of the time, Pallas kernels for 0%

profile of v1, /device:TPU:0, one launch (start us, length us, event | category | flops | bytes accessed | tf_op | source)
XLA Modules:
  0.0 1087.2 jit_solution(10209145720767926508)
XLA Ops:
  7.2 1.5 convert_reduce_fusion.2
  10.2 5.9 all-reduce.7
  16.0 12.6 %all-reduce.2 = (f32[4,256]{1,0:T(4,128)S(1)}, f32[4,256]{1,0:T(4,128)S(1)}) all-reduce(f32[4,256]{1,0:T(4,128)S(1)} %get-tuple-element.168, f32[4,256]{1,0:T(4,128)S(1)} %get-tuple-element.169), channel_id=1, replica_groups=mesh['dp'=4,'wide'=4,'narrow'=2] {'wide'}, use_global_device_ids=true, to_apply=%region_5.0 | all-reduce | flops 2048 | bytes 16384 | tf_op jit(solution)/shard_map/psum | solution.py:17
  28.7 2.2 add_convert_fusion
  31.0 19.6 %all-gather.6.cloned.1.call-done = bf16[4,256,512]{2,1,0:T(8,128)(2,1)} async-done(((bf16[4,256,256]{2,1,0:T(8,128)(2,1)}), bf16[4,256,512]{2,1,0:T(8,128)(2,1)}) %all-gather.6.cloned.1.call-update) | async-done | bytes 1048592 | tf_op jit(solution)/shard_map/all_gather | solution.py:149
  50.6 5.6 convolution_bitcast_fusion
  56.2 3.8 fusion.72
  60.7 72.4 %reduce-scatter.9.cloned.1.call-done = f32[1,256,1024]{2,1,0:T(8,128)} async-done(((f32[1,256,4096]{2,1,0:T(8,128)}), f32[1,256,1024]{2,1,0:T(8,128)}) %reduce-scatter.9.cloned.1.call-update) | async-done | bytes 1048592 | tf_op jit(solution)/shard_map/reduce_scatter | solution.py:154
  133.1 2.2 multiply_convert_fusion
  137.2 59.6 %reduce-scatter.7.cloned.1.call-done = f32[3,256,256]{2,1,0:T(8,128)} async-done(((f32[3,256,1024]{2,1,0:T(8,128)}), f32[3,256,256]{2,1,0:T(8,128)}) %reduce-scatter.7.cloned.1.call-update) | async-done | bytes 786448 | tf_op jit(solution)/shard_map/reduce_scatter | solution.py:153
  200.6 1.8 squeeze.37
  205.1 1.6 convert_element_type.95
  206.7 1.7 fusion.63
  210.2 22.1 %all_gather.19 = bf16[256,1024]{0,1:T(8,128)(2,1)} all-gather(bf16[256,256]{0,1:T(8,128)(2,1)S(1)} %bitcast.112), channel_id=1, replica_groups=mesh['dp'=4,'wide'=4,'narrow'=2] {'wide'}, dimensions={1}, use_global_device_ids=true | all-gather | bytes 655360 | tf_op jit(solution)/shard_map/all_gather | solution.py:172
  232.3 20.9 %all-gather.8.cloned.1.call-done = bf16[256,4096]{1,0:T(8,128)(2,1)} async-done(((bf16[256,1024]{1,0:T(8,128)(2,1)}), bf16[256,4096]{1,0:T(8,128)(2,1)}) %all-gather.8.cloned.1.call-update) | async-done | bytes 2097168 | tf_op jit(solution)/shard_map/all_gather | solution.py:173
  253.2 4.2 fusion.66
  258.8 2.1 convert_element_type.90
  262.0 3.7 fusion
  265.7 6.5 reduce-scatter.11.cloned.1.call-done
  272.2 1.8 multiply_reduce_fusion.6
  274.0 2.6 convolution_bitcast_fusion.2
  277.8 1.9 copy.142
  279.6 1.5 reshape.183
  281.1 1.6 fusion.29
  282.8 21.6 %all-reduce.19.cloned.1.call-done = (f32[256,52]{0,1:T(8,128)}, f32[256]{0:T(256)}, f32[256,52]{0,1:T(8,128)}) async-done(((f32[256,52]{0,1:T(8,128)}, f32[256]{0:T(256)}, f32[256,52]{0,1:T(8,128)}), (f32[256,52]{0,1:T(8,128)}, f32[256]{0:T(256)}, f32[256,52]{0,1:T(8,128)})) %all-reduce.19.cloned.1.call-update) | async-done | bytes 107536 | tf_op jit(solution)/shard_map/psum | solution.py:17
  305.9 35.8 %all-reduce.13.cloned.1.call-done = (f32[256,52]{0,1:T(8,128)}, f32[256]{0:T(256)}, f32[256,52]{0,1:T(8,128)}) async-done(((f32[256,52]{0,1:T(8,128)}, f32[256]{0:T(256)}, f32[256,52]{0,1:T(8,128)}), (f32[256,52]{0,1:T(8,128)}, f32[256]{0:T(256)}, f32[256,52]{0,1:T(8,128)})) %all-reduce.13.cloned.1.call-update) | async-done | bytes 107536 | tf_op jit(solution)/shard_map/psum | solution.py:17
  342.3 1.7 multiply_reduce_fusion.7
  345.1 1.7 convolution_add_fusion.1
  346.8 1.5 reshape.182
  349.6 1.5 copy.175
  351.1 2.4 fusion.34
  353.5 2.4 convert_reduce_fusion.3
  355.9 5.6 all_gather.21
  361.5 1.4 fusion.67
  363.1 5.5 fusion.69
  368.6 21.8 %reduce-scatter.13.cloned.1.call-done = f32[256,256]{1,0:T(8,128)} async-done(((f32[256,1024]{1,0:T(8,128)}), f32[256,256]{1,0:T(8,128)}) %reduce-scatter.13.cloned.1.call-update) | async-done | bytes 262160 | tf_op jit(solution)/shard_map/reduce_scatter | solution.py:227
  390.4 1.6 convert_element_type.107
  392.1 1.7 copy.178
  393.8 1.5 multiply_reduce_fusion.4
  401.5 1.8 pad_maximum_fusion.6
  405.1 2.0 convolution_convert_fusion
  408.2 2.4 convert_reduce_fusion.1
  410.6 58.2 %reduce-scatter.15.cloned.1.call-done = f32[256,1024]{1,0:T(8,128)} async-done(((f32[256,4096]{1,0:T(8,128)}), f32[256,1024]{1,0:T(8,128)}) %reduce-scatter.15.cloned.1.call-update) | async-done | bytes 1048592 | tf_op jit(solution)/shard_map/reduce_scatter | solution.py:230
  468.8 3.4 convert_reduce_fusion
  472.3 36.8 %all-gather.10.cloned.1.call-done = bf16[3,256,1024]{2,1,0:T(8,128)(2,1)} async-done(((bf16[3,256,256]{2,1,0:T(8,128)(2,1)}), bf16[3,256,1024]{2,1,0:T(8,128)(2,1)}) %all-gather.10.cloned.1.call-update) | async-done | bytes 1572880 | tf_op jit(solution)/shard_map/all_gather | solution.py:249
  509.1 3.6 fusion.68
  512.7 42.9 %all-gather.12.cloned.1.call-done = bf16[256,4096]{1,0:T(8,128)(2,1)} async-done(((bf16[256,1024]{1,0:T(8,128)(2,1)}), bf16[256,4096]{1,0:T(8,128)(2,1)}) %all-gather.12.cloned.1.call-update) | async-done | bytes 2097168 | tf_op jit(solution)/shard_map/all_gather | solution.py:250
  555.5 4.1 convolution_bitcast_fusion.1
  559.7 1.5 pad_maximum_fusion
  564.3 1.8 fusion.70
  566.2 4.7 fusion.71
  570.9 3.8 fusion.73
  574.7 17.2 %reduce-scatter.17.cloned.1.call-done = f32[4,256,256]{2,1,0:T(8,128)} async-done(((f32[4,256,512]{2,1,0:T(8,128)}), f32[4,256,256]{2,1,0:T(8,128)}) %reduce-scatter.17.cloned.1.call-update) | async-done | bytes 1048592 | tf_op jit(solution)/shard_map/reduce_scatter | solution.py:263
  591.9 2.6 multiply_reduce_fusion
  594.6 5.6 fusion.31
  602.1 3.3 convert_bitcast_fusion
  605.4 1.7 copy.161
  607.2 3.7 fusion.10
  611.8 5.0 all-reduce.5
  616.7 11.8 %all-reduce = (f32[4,256]{1,0:T(4,128)S(1)}, f32[4,256]{1,0:T(4,128)S(1)}) all-reduce(f32[4,256]{1,0:T(4,128)S(1)} %get-tuple-element.163, f32[4,256]{1,0:T(4,128)S(1)} %get-tuple-element.164), channel_id=1, replica_groups=mesh['dp'=4,'wide'=4,'narrow'=2] {'wide'}, use_global_device_ids=true, to_apply=%region_28.29 | all-reduce | flops 2048 | bytes 16384 | tf_op jit(solution)/shard_map/psum | solution.py:17
  630.3 427.4 %all-reduce.17.cloned.1.call-done = (f32[3,512,1024]{2,1,0:T(8,128)}, f32[1024,512]{1,0:T(8,128)}, f32[512,4096]{1,0:T(8,128)}, f32[4096,512]{1,0:T(8,128)}) async-done(((f32[3,512,1024]{2,1,0:T(8,128)}, f32[1024,512]{1,0:T(8,128)}, f32[512,4096]{1,0:T(8,128)}, f32[4096,512]{1,0:T(8,128)}), (f32[3,512,1024]{2,1,0:T(8,128)}, f32[1024,512]{1,0:T(8,128)}, f32[512,4096]{1,0:T(8,128)}, ...) | async-done | bytes 25165840 | tf_op jit(solution)/shard_map/psum | solution.py:275
  1057.6 7.1 copy.247
  1066.6 4.3 copy.250
  1072.7 3.9 copy.252
  (213 shorter events, 45.1 us)
Async XLA Ops:
  7.2 49.0 %copy-start = (bf16[3,512,1024]{2,1,0:T(8,128)(2,1)S(1)}, bf16[3,512,1024]{2,1,0:T(8,128)(2,1)}, u32[]{:S(2)}) copy-start(bf16[3,512,1024]{2,1,0:T(8,128)(2,1)} %param.21) | copy-start | bytes 9437188
  7.2 43.4 %all-gather.6.cloned.1.call-start = ((), (), s32[]{:S(2)}) async-start(), calls=%async_computation.6 | async-start | bytes 1572864 | tf_op jit(solution)/shard_map/all_gather | solution.py:149
  30.9 102.1 %reduce-scatter.9.cloned.1.call-start = ((), (), s32[]{:S(2)}) async-start(), calls=%async_computation.8 | async-start | bytes 5242880 | tf_op jit(solution)/shard_map/reduce_scatter | solution.py:154
  56.1 140.7 %reduce-scatter.7.cloned.1.call-start = ((), (), s32[]{:S(2)}) async-start(), calls=%async_computation.7 | async-start | bytes 3932160 | tf_op jit(solution)/shard_map/reduce_scatter | solution.py:153
  60.0 75.4 %copy-start.52 = (bf16[3,256]{1,0:T(4,128)(2,1)S(1)}, bf16[3,256]{1,0:T(4,128)(2,1)}, u32[]{:S(2)}) copy-start(bf16[3,256]{1,0:T(4,128)(2,1)} %param.22) | copy-start | bytes 4612
  60.0 193.2 %all-gather.8.cloned.1.call-start = ((), (), s32[]{:S(2)}) async-start(), calls=%async_computation.9 | async-start | bytes 2621440 | tf_op jit(solution)/shard_map/all_gather | solution.py:173
  60.7 138.0 %copy-start.41 = (f32[1024]{0:T(1024)}, f32[1024]{0:T(1024)S(1)}, u32[]{:S(2)}) copy-start(f32[1024]{0:T(1024)S(1)} %convert_element_type.100) | copy-start | bytes 12292
  135.3 136.9 %reduce-scatter.11.cloned.1.call-start = ((), (), s32[]{:S(2)}) async-start(), calls=%async_computation.10 | async-start | bytes 786432 | tf_op jit(solution)/shard_map/reduce_scatter | solution.py:179
  206.7 1.7 copy-start.32
  206.7 1.9 copy-start.26
  206.7 2.0 copy-start.28
  206.7 2.0 copy-start.36
  208.6 1.5 copy-start.17
  208.6 1.5 copy-start.19
  253.2 4.2 copy-start.6
  253.2 4.2 copy-start.11
  257.4 3.5 copy-start.55
  257.4 4.0 copy-start.56
  258.7 45.7 %all-reduce.19.cloned.1.call-start = ((), (), s32[]{:S(2)}) async-start(), calls=%async_computation.19 | async-start | bytes 231424 | tf_op jit(solution)/shard_map/psum | solution.py:17
  272.2 4.4 copy-start.33
  274.0 79.5 %copy-start.9 = (f32[256,256]{1,0:T(8,128)}, f32[256,256]{1,0:T(8,128)S(1)}, u32[]{:S(2)}) copy-start(f32[256,256]{1,0:T(8,128)S(1)} %get-tuple-element.178) | copy-start | bytes 786436
  282.8 58.9 %all-reduce.13.cloned.1.call-start = ((), (), s32[]{:S(2)}) async-start(), calls=%async_computation.16 | async-start | bytes 231424 | tf_op jit(solution)/shard_map/psum | solution.py:17
  304.5 86.0 %reduce-scatter.13.cloned.1.call-start = ((), (), s32[]{:S(2)}) async-start(), calls=%async_computation.11 | async-start | bytes 1310720 | tf_op jit(solution)/shard_map/reduce_scatter | solution.py:227
  342.3 2.8 copy-start.44
  351.1 10.5 copy-start.12
  363.0 105.8 %reduce-scatter.15.cloned.1.call-start = ((), (), s32[]{:S(2)}) async-start(), calls=%async_computation.13 | async-start | bytes 5242880 | tf_op jit(solution)/shard_map/reduce_scatter | solution.py:230
  368.6 140.5 %all-gather.10.cloned.1.call-start = ((), (), s32[]{:S(2)}) async-start(), calls=%async_computation.12 | async-start | bytes 1966080 | tf_op jit(solution)/shard_map/all_gather | solution.py:249
  393.7 2.7 copy-start.22
  393.7 2.7 copy-start.24
  393.7 2.7 copy-start.29
  393.7 3.2 copy-start.18
  393.7 3.2 copy-start.20
  393.7 3.2 copy-start.27
  395.2 2.9 copy-start.31
  410.6 145.0 %all-gather.12.cloned.1.call-start = ((), (), s32[]{:S(2)}) async-start(), calls=%async_computation.15 | async-start | bytes 2621440 | tf_op jit(solution)/shard_map/all_gather | solution.py:250
  472.3 119.7 %reduce-scatter.17.cloned.1.call-start = ((), (), s32[]{:S(2)}) async-start(), calls=%async_computation.14 | async-start | bytes 3145728 | tf_op jit(solution)/shard_map/reduce_scatter | solution.py:263
  512.7 47.0 %copy-start.5 = (f32[3,256,512]{2,1,0:T(8,128)S(1)}, f32[3,256,512]{2,1,0:T(8,128)}, u32[]{:S(2)}) copy-start(f32[3,256,512]{2,1,0:T(8,128)} %fusion.68) | copy-start | bytes 4718596
  561.2 2.3 copy-start.10
  561.2 2.3 copy-start.39
  561.2 2.3 copy-start.46
  561.2 3.2 copy-start.7
  561.2 5.0 copy-start.13
  561.2 69.0 %all-reduce.15.cloned.1.call-start = ((), (), s32[]{:S(2)}) async-start(), calls=%async_computation.17 | async-start | bytes 209920 | tf_op jit(solution)/shard_map/psum | solution.py:275
  566.2 4.7 copy-start.16
  566.2 4.7 copy-start.34
  570.9 21.0 %copy-start.3 = (bf16[4,256,256]{2,1,0:T(8,128)(2,1)S(1)}, bf16[4,256,256]{2,1,0:T(8,128)(2,1)}, u32[]{:S(2)}) copy-start(bf16[4,256,256]{2,1,0:T(8,128)(2,1)} %param.18) | copy-start | bytes 1572868
  570.9 23.7 %copy-start.15 = (bf16[256,4096]{1,0:T(8,128)(2,1)S(1)}, bf16[256,4096]{1,0:T(8,128)(2,1)}, u32[]{:S(2)}) copy-start(bf16[256,4096]{1,0:T(8,128)(2,1)} %all-gather.12.cloned.1.call-done) | copy-start | bytes 6291460
  594.6 463.1 %all-reduce.17.cloned.1.call-start = ((), (), s32[]{:S(2)}) async-start(), calls=%async_computation.18 | async-start | bytes 50331648 | tf_op jit(solution)/shard_map/psum | solution.py:275
  607.2 21.4 %copy-start.8 = (f32[4,256,256]{2,1,0:T(8,128)S(1)}, f32[4,256,256]{2,1,0:T(8,128)}, u32[]{:S(2)}) copy-start(f32[4,256,256]{2,1,0:T(8,128)} %reduce-scatter.17.cloned.1.call-done) | copy-start | bytes 3145732
  610.9 18.4 %copy-start.30 = (f32[256,256]{1,0:T(8,128)S(1)}, f32[256,256]{1,0:T(8,128)}, u32[]{:S(2)}) copy-start(f32[256,256]{1,0:T(8,128)} %get-tuple-element.172) | copy-start | bytes 786436
  1057.6 7.1 copy-start.50
  1057.6 7.7 copy-start.14
  1057.6 9.0 copy-start.4
  1065.3 6.2 slice-start
  1066.6 4.3 copy-start.49
  1066.6 6.0 slice-start.1
  1072.6 4.0 copy-start.54
  1072.6 4.5 copy-start.48
  1072.6 5.1 copy-start.47
  1072.6 5.7 copy-start.53
  1072.6 6.3 copy-start.40
  1072.6 6.9 copy-start.43
  1072.7 7.5 copy-start.57
  1072.7 8.0 copy-start.1
  (10 other events, 11.2 us)
Sparse Core Ops, SparseCore 0:
  31.0 19.4 all-gather.5
  56.3 76.7 reduce-scatter.8
  136.1 60.7 reduce-scatter.6
  198.9 54.2 all-gather.7
  258.8 13.3 reduce-scatter.10
  282.9 21.4 all-reduce.18
  307.0 34.6 all-reduce.12
  363.1 27.2 reduce-scatter.12
  393.3 75.4 reduce-scatter.14
  470.9 38.1 all-gather.9
  511.3 44.1 all-gather.11
  561.3 30.5 reduce-scatter.16
  596.1 30.8 all-reduce.14
  631.0 426.6 all-reduce.16
